TPU v7x, 512 devices: a whole 4x4x16 slice. The times are simulated.
512 devices in a mesh: grp: 8 (over x, core), seq: 16 (over z), voc: 4 (over y).
Axes of the slice: x: 4, y: 4, z: 16, core: 2. Of those that a mesh axis runs over, the one named last changes fastest.
Arguments:
- prompt_kv: bfloat16 [8, 2048, 1024], P('grp', 'seq', 'voc'), may hold values from -6 to 6
- owner: int32 [8, 16], P('grp'), may hold values from 0 to 7, as said below
- queries: bfloat16 [8, 16, 64, 4096], P('grp', 'seq', None, 'voc'), may hold values from -120 to 120
- resp_kv: bfloat16 [8, 16, 64, 1024], P('grp', 'seq', None, 'voc'), may hold values from -6 to 6
- lengths: int32 [8, 16], P('grp', 'seq'), may hold values from 1 to 64, as said below
- out_proj: bfloat16 [4096, 5120], P('voc', 'seq'), may hold values from -0.09375 to 0.09375
- resid: bfloat16 [8, 16, 64, 5120], P('grp', 'seq'), may hold values from -6 to 6
- gain: bfloat16 [5120], replicated, may hold values from 0.5 to 1.5
- head_w: bfloat16 [1024, 5120], P('voc'), may hold values from -4 to 4
- token_ids: int32 [8, 16, 64], P('grp', 'seq'), may hold values from 0 to 1023
- pol_logprobs: float32 [8, 16, 64], P('grp', 'seq'), may hold values from -9 to -5
Outputs:
- ref_logprobs: float32 [8, 16, 64], P('grp', 'seq')
- token_kl: float32 [8, 16, 64], P('grp', 'seq')
Inputs may be any that keep to these rules, and one draw needn't show every extreme that they name: `owner`: every prompt index names exactly 16 responses. `lengths`: some response has exactly 64 valid tokens.
All inputs are finite; a program needn't handle non-finite values.
Results may differ from a plain program's by a relative error of at most 0.004.
Values may be sent and summed in bfloat16 or wider, within the bound.
A program may use at most 64 MiB of HBM per device.

v0:
```python
import math

import jax
import jax.numpy as jnp
from jax import lax
from jax.sharding import PartitionSpec as P

HD = 128
QPK = 8
RT = 64
VOC_DEV = 256


def combined_all(value, axis, join):
    pieces = jax.tree.map(lambda part: lax.all_gather(part, axis), value)
    head = jax.tree.map(lambda part: part[0], pieces)
    tail = jax.tree.map(lambda part: part[1:], pieces)
    so_far, _ = lax.scan(lambda so_far, piece: (join(so_far, piece), None), head, tail)
    return so_far


def attend(query_rows, key_rows, value_rows, positions, prompt_len):
    scores = lax.dot_general(
        query_rows, key_rows, (((1,), (1,)), ((), ())), preferred_element_type=jnp.float32
    )
    scores = scores * (1.0 / math.sqrt(query_rows.shape[1]))
    columns = jnp.arange(key_rows.shape[0], dtype=jnp.int32)
    visible = (columns[None, :] < prompt_len) | (
        columns[None, :] - prompt_len <= positions[:, None]
    )
    scores = jnp.where(visible, scores, -jnp.inf)
    highest = jnp.max(scores, axis=1, keepdims=True)
    weights = jnp.exp(scores - highest)
    weights = (weights / jnp.sum(weights, axis=1, keepdims=True)).astype(jnp.bfloat16)
    return jnp.dot(weights, value_rows, preferred_element_type=jnp.float32).astype(jnp.bfloat16)


def combine_stats(first, second):
    highest = jnp.maximum(first[0], second[0])
    exp_total = first[1] * jnp.exp(first[0] - highest) + second[1] * jnp.exp(second[0] - highest)
    return (highest, exp_total, first[2] + second[2])


def rms_normed(resid_rows, summed, gain):
    hidden = resid_rows.astype(jnp.float32) + summed
    scale = lax.rsqrt(jnp.mean(hidden * hidden, axis=1, keepdims=True) + 1e-06)
    return (hidden * scale * gain.astype(jnp.float32)[None, :]).astype(jnp.bfloat16)


def local(
    prompt_kv,
    owner,
    queries,
    resp_kv,
    lengths,
    out_proj,
    resid,
    gain,
    head_w,
    token_ids,
    pol_logprobs,
):
    pieces = lax.all_gather(prompt_kv, "grp", axis=0, tiled=True)
    chosen = jnp.take(pieces, owner[0], axis=0)
    routed = lax.all_to_all(chosen, "seq", split_axis=0, concat_axis=0, tiled=True)
    prompt_len = routed.shape[0] * routed.shape[1]
    flat_rows = routed.reshape(prompt_len, 2 * HD)
    own_rows = resp_kv[0, 0]
    key_rows = jnp.concatenate([flat_rows[:, :HD], own_rows[:, :HD]], axis=0)
    value_rows = jnp.concatenate([flat_rows[:, HD:], own_rows[:, HD:]], axis=0)
    query_rows = queries[0, 0].reshape(RT, QPK, HD).transpose(1, 0, 2).reshape(QPK * RT, HD)
    positions = jnp.tile(jnp.arange(RT, dtype=jnp.int32), QPK)
    row_total = QPK * RT
    per_block = min(row_total, 512)
    block_count = row_total // per_block

    def attend_block(item):
        return attend(item[0], key_rows, value_rows, item[1], prompt_len)

    blocks_out = lax.map(
        attend_block,
        (query_rows.reshape(block_count, per_block, HD), positions.reshape(block_count, per_block)),
    )
    attention = blocks_out.reshape(QPK, RT, HD).transpose(1, 0, 2).reshape(RT, QPK * HD)
    partial_sum = jnp.dot(
        attention,
        lax.all_gather(out_proj, "seq", axis=1, tiled=True),
        preferred_element_type=jnp.float32,
    )
    branch = lax.psum(partial_sum, "voc")
    normed = rms_normed(resid[0, 0], branch, gain)
    logits = lax.dot_general(
        normed, head_w, (((1,), (1,)), ((), ())), preferred_element_type=jnp.float32
    )
    vocab_start = lax.axis_index("voc") * VOC_DEV
    local_high = jnp.max(logits, axis=1)
    local_total = jnp.sum(jnp.exp(logits - local_high[:, None]), axis=1)
    matches = (
        token_ids[0, 0][:, None] - vocab_start == jnp.arange(VOC_DEV, dtype=jnp.int32)[None, :]
    )
    picked = jnp.sum(jnp.where(matches, logits, 0.0), axis=1)
    highest, exp_total, target = combined_all(
        (local_high, local_total, picked), "voc", combine_stats
    )
    ref_logprob = target - (highest + jnp.log(exp_total))
    live_rows = jnp.arange(RT, dtype=jnp.int32) < lengths[0, 0]
    delta = jnp.clip(ref_logprob - pol_logprobs[0, 0], -20.0, 20.0)
    divergence = jnp.clip(jnp.exp(delta) - delta - 1.0, -10.0, 10.0)
    zeros = jnp.zeros_like(ref_logprob)
    return (
        jnp.where(live_rows, ref_logprob, zeros)[None, None],
        jnp.where(live_rows, divergence, zeros)[None, None],
    )


def solution(mesh):
    in_specs = (
        P("grp", "seq", "voc"),
        P("grp", None),
        P("grp", "seq", None, "voc"),
        P("grp", "seq", None, "voc"),
        P("grp", "seq"),
        P("voc", "seq"),
        P("grp", "seq", None, None),
        P(),
        P("voc", None),
        P("grp", "seq", None),
        P("grp", "seq", None),
    )
    out_specs = (P("grp", "seq", None), P("grp", "seq", None))
    return jax.shard_map(local, mesh=mesh, in_specs=in_specs, out_specs=out_specs, check_vma=False)
```

profile of v0, /device:TPU:1, one launch (start us, length us, event | category | flops | bytes accessed | tf_op | source)
XLA Modules:
  0.0 275.7 jit_solution(900582078785323184)
XLA Ops:
  7.2 0.7 all-gather.5.cloned.1.call-update
  7.9 0.7 fusion.29
  8.6 20.0 %all_gather.24 = bf16[8,128,256]{2,1,0:T(8,128)(2,1)S(1)} all-gather(bf16[1,128,256]{2,1,0:T(8,128)(2,1)} %param.13), channel_id=1, replica_groups=mesh['grp'=8,'seq'=16,'voc'=4] {'grp'}, dimensions={0}, use_global_device_ids=true | all-gather | bytes 589824 | tf_op jit(solution)/shard_map/all_gather | solution.py:63
  28.7 1.6 gather_fusion
  30.3 2.4 broadcast_select_fusion
  32.6 9.9 %all-to-all-start = ((bf16[16,128,256]{2,1,0:T(8,128)(2,1)}), bf16[16,128,256]{2,1,0:T(8,128)(2,1)}, u32[]{:S(2)}, u32[]{:S(2)}) async-start(bf16[16,128,256]{2,1,0:T(8,128)(2,1)} %broadcast_select_fusion), calls=%async_computation | async-start | bytes 2097152 | tf_op jit(solution)/shard_map/all_to_all | solution.py:65
  42.7 0.1 le.30
  42.8 59.9 %all-to-all-done = bf16[16,128,256]{2,1,0:T(8,128)(2,1)} async-done(((bf16[16,128,256]{2,1,0:T(8,128)(2,1)}), bf16[16,128,256]{2,1,0:T(8,128)(2,1)}, u32[]{:S(2)}, u32[]{:S(2)}) %all-to-all-start) | async-done | bytes 1048608 | tf_op jit(solution)/shard_map/all_to_all | solution.py:65
  102.7 1.3 fusion.34
  104.0 1.2 fusion.36
  105.1 0.7 fusion.9
  105.8 0.9 fusion.11
  106.7 0.1 copy.17
  106.8 80.6 %all-gather.5.cloned.1.call-done = bf16[1024,5120]{0,1:T(8,128)(2,1)} async-done(((bf16[1024,320]{0,1:T(8,128)(2,1)}), bf16[1024,5120]{0,1:T(8,128)(2,1)}) %all-gather.5.cloned.1.call-update) | async-done | bytes 10485776 | tf_op jit(solution)/shard_map/all_gather | solution.py:87
  187.4 8.4 %fusion.22 = f32[64,5120]{1,0:T(8,128)} fusion(bf16[1024,5120]{0,1:T(8,128)(2,1)} %all-gather.5.cloned.1.call-done, bf16[8,8,8,128]{3,2,1,0:T(8,128)(2,1)S(1)} %bitcast.71), kind=kOutput, calls=%fused_computation.33 | convolution fusion | flops 671088640 | bytes 11927552 | tf_op jit(solution)/shard_map/dot_general | solution.py:85
  196.5 1.3 dynamic-slice
  198.5 57.4 %all-reduce.6.cloned.1.call-done = f32[64,5120]{1,0:T(8,128)} async-done(((f32[64,5120]{1,0:T(8,128)}), f32[64,5120]{1,0:T(8,128)}) %all-reduce.6.cloned.1.call-update) | async-done | bytes 1310736 | tf_op jit(solution)/shard_map/psum | solution.py:90
  255.9 1.7 multiply_reduce_fusion
  257.6 1.0 fusion.37
  258.7 0.2 select_reduce_fusion
  258.9 0.2 dynamic-update-slice
  259.1 0.2 dynamic-update-slice.2
  259.3 0.2 dynamic-update-slice.1
  259.5 8.2 %all-reduce.3 = (f32[256]{0:T(256)S(1)}, f32[256]{0:T(256)S(1)}, f32[256]{0:T(256)S(1)}) all-reduce(f32[256]{0:T(256)S(1)} %dynamic-update-slice, f32[256]{0:T(256)S(1)} %dynamic-update-slice.1, f32[256]{0:T(256)S(1)} %dynamic-update-slice.2), channel_id=2, replica_groups=mesh['grp'=8,'seq'=16,'voc'=4] {'voc'}, use_global_device_ids=true, to_apply=%add | all-reduce | flops 768 | bytes 6144
  267.7 0.1 slice.43
  267.8 0.1 slice.44
  267.9 0.1 slice.45
  268.0 0.1 reshape.106
  268.0 0.1 reshape.107
  268.1 0.1 reshape.108
  268.2 0.1 while.4
  268.3 0.5 fusion.28
  (41 shorter events, 0.3 us)
Async XLA Ops:
  7.2 250.4 %copy-start = (bf16[256,5120]{1,0:T(8,128)(2,1)S(1)}, bf16[256,5120]{1,0:T(8,128)(2,1)}, u32[]{:S(2)}) copy-start(bf16[256,5120]{1,0:T(8,128)(2,1)} %param.21) | copy-start | bytes 7864324
  7.2 23.1 %copy-start.7 = (s32[1,16]{1,0:T(1,128)S(1)}, s32[1,16]{1,0:T(1,128)}, u32[]{:S(2)}) copy-start(s32[1,16]{1,0:T(1,128)} %param.14) | copy-start | bytes 196
  7.2 180.2 %all-gather.5.cloned.1.call-start = ((), (), s32[]{:S(2)}) async-start(), calls=%async_computation.1 | async-start | bytes 11141120 | tf_op jit(solution)/shard_map/all_gather | solution.py:87
  30.2 12.4 %copy-start.3 = (bf16[1,1,64,1024]{3,2,1,0:T(8,128)(2,1)S(1)}, bf16[1,1,64,1024]{3,2,1,0:T(8,128)(2,1)}, u32[]{:S(2)}) copy-start(bf16[1,1,64,1024]{3,2,1,0:T(8,128)(2,1)} %param.15) | copy-start | bytes 393220
  30.2 12.6 %copy-start.4 = (bf16[1,1,64,256]{3,2,1,0:T(8,128)(2,1)S(1)}, bf16[1,1,64,256]{3,2,1,0:T(8,128)(2,1)}, u32[]{:S(2)}) copy-start(bf16[1,1,64,256]{3,2,1,0:T(8,128)(2,1)} %param.16) | copy-start | bytes 98308
  32.6 70.0 %all-to-all-start = ((bf16[16,128,256]{2,1,0:T(8,128)(2,1)}), bf16[16,128,256]{2,1,0:T(8,128)(2,1)}, u32[]{:S(2)}, u32[]{:S(2)}) async-start(bf16[16,128,256]{2,1,0:T(8,128)(2,1)} %broadcast_select_fusion), calls=%async_computation | async-start | bytes 2097152 | tf_op jit(solution)/shard_map/all_to_all | solution.py:65
  42.6 213.3 %all-reduce.6.cloned.1.call-start = ((), (), s32[]{:S(2)}) async-start(), calls=%async_computation.2 | async-start | bytes 2621440 | tf_op jit(solution)/shard_map/psum | solution.py:90
  187.4 8.5 %copy-start.5 = (bf16[5120]{0:T(1024)(128)(2,1)S(1)}, bf16[5120]{0:T(1024)(128)(2,1)}, u32[]{:S(2)}) copy-start(bf16[5120]{0:T(1024)(128)(2,1)} %param.20) | copy-start | bytes 30724
  187.4 11.1 %copy-start.8 = (s32[1,1,64]{2,1,0:T(1,128)S(1)}, s32[1,1,64]{2,1,0:T(1,128)}, u32[]{:S(2)}) copy-start(s32[1,1,64]{2,1,0:T(1,128)} %param.22) | copy-start | bytes 772
  187.4 68.5 %copy-start.2 = (bf16[1,1,64,5120]{3,2,1,0:T(8,128)(2,1)S(1)}, bf16[1,1,64,5120]{3,2,1,0:T(8,128)(2,1)}, u32[]{:S(2)}) copy-start(bf16[1,1,64,5120]{3,2,1,0:T(8,128)(2,1)} %param.19) | copy-start | bytes 1966084
  255.9 1.7 copy-start.1
  257.6 10.8 %copy-start.6 = (f32[1,1,64]{2,1,0:T(1,128)S(1)}, f32[1,1,64]{2,1,0:T(1,128)}, u32[]{:S(2)}) copy-start(f32[1,1,64]{2,1,0:T(1,128)} %param.23) | copy-start | bytes 772
Sparse Core Ops, SparseCore 0:
  10.1 177.2 all-gather.4
  196.0 59.8 all-reduce.5
where the time goes:
time: 278 us; the launch traced here: 276 us
  waiting for transfers between devices  199 us (72%)
  blocking collectives  28.2 us (10%)
  between operations  15.6 us (6%)
  matrix products  11.5 us (4%)
  starting transfers between devices  10 us (4%)
  other arithmetic  6.29 us (2%)
  local copies, waits for them, and re-layouts  5.5 us (2%)
    all_gather x1, waiting for transfers between devices, local(): lax.all_gather(out_proj, 'seq', axis=1, tiled=True)  80.6 us
    all_to_all x1, waiting for transfers between devices, local(): lax.all_to_all(chosen, 'seq', split_axis=0, concat_axis=0, tiled=True)  59.9 us
    psum x1, waiting for transfers between devices, local(): branch = lax.psum(partial_sum, 'voc')  57.4 us
    all_gather x1, blocking collectives, local(): pieces = lax.all_gather(prompt_kv, 'grp', axis=0, tiled=True)  20 us
    all_to_all x1, starting transfers between devices, local(): lax.all_to_all(chosen, 'seq', split_axis=0, concat_axis=0, tiled=True)  9.94 us
    dot_general x1, matrix products, local(): jnp.dot(attention, lax.all_gather(out_proj, 'seq', axis=1, tiled=True), p...  8.42 us
    unnamed x1, blocking collectives  8.22 us
  transfers between devices with their start and end apart: 3, of which 3 were waited for; matrix products, arithmetic and copies ran while one was open for 4% of the time, Pallas kernels for 0%

commit v1 on v0

v1 whole, which is shorter than its diff:
```python
import functools
import math

import jax
import jax.numpy as jnp
from jax import lax
from jax.experimental import pallas as pl
from jax.experimental.pallas import tpu as pltpu
from jax.sharding import PartitionSpec as P

MESH = pl.DeviceIdType.MESH
HD = 128
RT = 64
D = 5120
CW = 640
NCH = D // CW
BF = jnp.bfloat16
F32 = jnp.float32
LOG2E_SCALE = math.log2(math.e) / math.sqrt(HD)
CHUNKS = ((0, 1, 2), (3, 4, 5, 6), (7, 8, 9, 10), (11, 12, 13, 14, 15))
STARTS = (0, 512, 1024, 1536, 2176)
PLACE = {slot: (t, i) for t, slots in enumerate(CHUNKS) for i, slot in enumerate(slots)}


def slot_of(way, hop):
    return 0 if hop == 0 else 15 if hop == 8 else 2 * hop - 1 + way


def lanes_max(rows):
    high = jnp.abs(rows[:, 0:128])
    for i in range(128, rows.shape[1], 128):
        high = jnp.maximum(high, jnp.abs(rows[:, i : i + 128]))
    return jnp.broadcast_to(jnp.max(high, axis=1, keepdims=True), high.shape)


def encode(rows):
    exponent = jnp.ceil(jnp.log2(jnp.maximum(lanes_max(rows), 1e-30)) + 0.01)
    scale = jnp.exp2(-exponent) * 32000.0
    scaled = rows * jnp.concatenate([scale] * (CW // 128), axis=1)
    return jnp.concatenate([jnp.round(scaled), exponent], axis=1).astype(jnp.int16)


def decode(coded):
    scale = jnp.exp2(coded[:, CW:].astype(F32)) * (1.0 / 32000.0)
    return coded[:, :CW].astype(F32) * jnp.concatenate([scale] * (CW // 128), axis=1)


def kernel(
    kv_ref, owner_ref, q_ref, own_ref, len_ref, proj_ref, resid_ref, gain_ref, head_ref, tok_ref, pol_ref,
    ref_out, kl_out,
    kv0, kv1, kv2, kv3, packs, own_blocks, owner_in, owner_v, owner_s, m_s, l_s, probs, att_send, att_recv, att,
    v_in, w_slots, core_send, core_recv, tmp1, own1, send1, recv1, tmp2, own2, send2, recv2,
    resid_v, head_v, gain_v, tok_v, pol_v, len_s, hidden_c, squares, stats, load_sem,
    q_ss, q_rs, o_ss, o_rs, kv_ss, kv_rs, sib_ss, sib_rs, w_ss, w_rs, a_ss, a_rs, c_ss, c_rs,
    f_ss, f_rs, g_ss, g_rs, n_ss, n_rs, t_ss, t_rs, e_ss, e_rs,
):
    g, s, v = lax.axis_index("grp"), lax.axis_index("seq"), lax.axis_index("voc")
    x, c = lax.div(g, 2), lax.rem(g, 2)
    kvs = (kv0, kv1, kv2, kv3)
    sends = []

    def remote(src, dst, ss, rs, device):
        return pltpu.make_async_remote_copy(
            src_ref=src, dst_ref=dst, send_sem=ss, recv_sem=rs, device_id=device, device_id_type=MESH
        )

    def launch(copy):
        copy.start()
        sends.append(copy)

    def grp(d):
        return {"grp": lax.rem(g + d, 8)}

    def along_x(d):
        return {"grp": lax.rem(g + 2 * d, 8)}

    def along_y(d):
        return {"voc": lax.rem(v + d, 4)}

    def along_z(way):
        return {"seq": lax.rem(s + (1 if way == 0 else 15), 16)}

    sibling = {"grp": 2 * x + 1 - c}

    barrier = pltpu.get_barrier_semaphore()
    for device in [grp(d) for d in range(1, 8)] + [along_y(d) for d in range(1, 4)] + [along_z(0), along_z(1)]:
        pl.semaphore_signal(barrier, inc=1, device_id=device, device_id_type=MESH)

    def load(index, src, dst):
        copy = pltpu.make_async_copy(src, dst, load_sem.at[index])
        copy.start()
        return copy

    early = [
        load(0, owner_ref, owner_in),
        load(1, kv_ref.at[0, :, pl.ds(HD, HD)], v_in),
        load(2, kv_ref.at[0, :, pl.ds(0, HD)], kv0.at[c, 0, pl.ds(0, HD)]),
    ]
    early += [load(3 + j, q_ref.at[0, 0, :, pl.ds(j * HD, HD)], packs.at[x, pl.ds(j * RT, RT)]) for j in range(8)]
    early += [load(11 + j, own_ref.at[0, 0, :, pl.ds(j * HD, HD)], packs.at[x, pl.ds(512 + j * RT, RT)]) for j in range(2)]
    early.append(load(13, proj_ref.at[:, pl.ds(pl.multiple_of(g * HD, HD), HD)], w_slots.at[s]))
    late = [
        load(14, resid_ref.at[0, 0, pl.ds(pl.multiple_of(v * 16, 16), 16), :], resid_v),
        load(15, head_ref, head_v),
        load(16, gain_ref, gain_v),
        load(17, tok_ref, tok_v),
        load(18, pol_ref, pol_v),
        load(19, len_ref, len_s),
    ]
    for copy in early:
        copy.wait()
    kv0[c, 0, 128:256] = v_in[...].T
    owner_v[pl.ds(g, 1), :] = jnp.full((1, 128), owner_in[0, s], jnp.int32)

    pl.semaphore_wait(barrier, 12)

    def kv_piece(slot, sub):
        t, i = PLACE[slot]
        return kvs[t].at[c, i, pl.ds(sub * 128, 128)]

    def kv_copy(way, hop, sub):
        return remote(
            kv_piece(slot_of(way, hop - 1), sub), kv_piece(slot_of(way, hop), sub),
            kv_ss.at[way, hop - 1, sub], kv_rs.at[way, hop - 1, sub], along_z(way),
        )

    def kv_subs(way, hop):
        return (0, 1) if hop < 8 else (way,)

    def sib_copy(slot):
        t, i = PLACE[slot]
        return remote(kvs[t].at[c, i], kvs[t].at[c, i], sib_ss.at[slot], sib_rs.at[slot], sibling)

    def kv_hop(hop):
        for sub in (0, 1):
            for way in (0, 1):
                if sub in kv_subs(way, hop):
                    kv_copy(way, hop, sub).wait_recv()
                    if hop < 8 and sub in kv_subs(way, hop + 1):
                        launch(kv_copy(way, hop + 1, sub))
        for slot in sorted({slot_of(0, hop), slot_of(1, hop)}):
            launch(sib_copy(slot))

    def w_piece(way, hop, which):
        index = lax.rem(s + (16 - hop if way == 0 else hop), 16)
        if which == 8:
            return w_slots.at[index, pl.ds(way * 160, 160)]
        return w_slots.at[index]

    def w_copy(way, hop):
        return remote(
            w_piece(way, hop - 1, hop), w_piece(way, hop - 1, hop), w_ss.at[way, hop - 1], w_rs.at[way, hop - 1],
            along_z(way),
        )

    def w_arrived(way, hop):
        ref = w_piece(way, hop, hop)
        return remote(ref, ref, w_ss.at[way, hop - 1], w_rs.at[way, hop - 1], along_z(way))

    def w_hop(hop):
        for way in (0, 1):
            w_arrived(way, hop).wait_recv()
            if hop < 8:
                launch(w_copy(way, hop + 1))

    for sub in (0, 1):
        for way in (0, 1):
            launch(kv_copy(way, 1, sub))
    launch(sib_copy(0))
    for d in range(1, 8):
        row = owner_v.at[pl.ds(g, 1)]
        launch(remote(row, row, o_ss.at[d - 1], o_rs.at[d - 1], grp(d)))
    for d in (1, 3, 2):
        launch(remote(packs.at[x], packs.at[x], q_ss.at[d - 1], q_rs.at[d - 1], along_x(d)))

    kv_hop(1)
    kv_hop(2)

    for d in range(1, 8):
        row = owner_v.at[pl.ds(lax.rem(g + 8 - d, 8), 1)]
        remote(row, row, o_ss.at[d - 1], o_rs.at[d - 1], grp(d)).wait_recv()
    to_scalar = pltpu.make_async_copy(owner_v, owner_s, load_sem.at[20])
    to_scalar.start()
    for d in (1, 3, 2):
        ref = packs.at[lax.rem(x + 4 - d, 4)]
        remote(ref, ref, q_ss.at[d - 1], q_rs.at[d - 1], along_x(d)).wait_recv()
    to_scalar.wait()
    pad = jnp.zeros((64, 128), BF)
    for u in range(4):
        own_blocks[u, 0:64] = packs[u, 512:576]
        own_blocks[u, 64:128] = pad
        own_blocks[u, 128:256] = jnp.concatenate([packs[u, 576:640], pad], axis=0).T

    def attend(t, units):
        n = len(CHUNKS[t])
        for u in units:
            odd_prompt = lax.rem(owner_s[2 * u + c, 0], 2)
            keys = [kvs[t][odd_prompt, i, 0:128] for i in range(n)]
            if t == 0:
                keys.append(own_blocks[u, 0:128])
            keys = jnp.concatenate(keys, axis=0)
            scores = lax.dot_general(
                keys, packs[u, 0:512], (((1,), (1,)), ((), ())), preferred_element_type=F32
            )
            if t == 0:
                row = lax.broadcasted_iota(jnp.int32, (128, 512), 0)
                position = lax.broadcasted_iota(jnp.int32, (128, 512), 1) & 63
                mine = jnp.where(row <= position, scores[n * 128 :], -1e30)
                scores = jnp.concatenate([scores[: n * 128], mine], axis=0)
            high = jnp.max(scores, axis=0, keepdims=True) * LOG2E_SCALE
            if t > 0:
                before = m_s[u, t - 1 : t]
                high = jnp.maximum(before, high)
            weights = jnp.exp2(scores * LOG2E_SCALE - high)
            total = jnp.sum(weights, axis=0, keepdims=True)
            if t > 0:
                total = l_s[u, 0:1] * jnp.exp2(before - high) + total
            m_s[u, t : t + 1] = high
            l_s[u, 0:1] = total
            probs[u, STARTS[t] : STARTS[t + 1]] = weights

    def weigh(u):
        odd_prompt = lax.rem(owner_s[2 * u + c, 0], 2)
        last, inverse = m_s[u, 3:4], 1.0 / l_s[u, 0:1]
        out = jnp.zeros((128, 512), F32)
        for t in range(4):
            values = [kvs[t][odd_prompt, i, 128:256] for i in range(len(CHUNKS[t]))]
            if t == 0:
                values.append(own_blocks[u, 128:256])
            share = jnp.exp2(m_s[u, t : t + 1] - last) * inverse
            weights = (probs[u, STARTS[t] : STARTS[t + 1]] * share).astype(BF)
            out = out + jnp.dot(jnp.concatenate(values, axis=1), weights, preferred_element_type=F32)
        att_send[u] = out.T.astype(BF)

    def chunk_ready(t):
        for slot in CHUNKS[t]:
            sib_ref = kvs[t].at[1 - c, PLACE[slot][1]]
            remote(sib_ref, sib_ref, sib_ss.at[slot], sib_rs.at[slot], sibling).wait_recv()

    for way in (0, 1):
        launch(w_copy(way, 1))
    kv_hop(3)
    chunk_ready(0)
    attend(0, (0, 1))
    kv_hop(4)
    attend(0, (2, 3))
    w_hop(1)
    kv_hop(5)
    chunk_ready(1)
    attend(1, (0, 1))
    w_hop(2)
    kv_hop(6)
    attend(1, (2, 3))
    w_hop(3)
    kv_hop(7)
    chunk_ready(2)
    attend(2, (0, 1))
    w_hop(4)
    kv_hop(8)
    attend(2, (2, 3))
    w_hop(5)
    chunk_ready(3)
    attend(3, (0, 1))
    w_hop(6)
    attend(3, (2, 3))

    for u in range(4):
        weigh(u)
    for d in (1, 2, 3, 5, 6, 7, 4):
        j = lax.rem(g + d, 8)
        launch(remote(
            att_send.at[:, pl.ds(pl.multiple_of(j * RT, RT), RT), :], att_recv.at[x, c],
            a_ss.at[d - 1], a_rs.at[d - 1], grp(d),
        ))
    att_recv[x, c] = att_send[:, pl.ds(pl.multiple_of(g * RT, RT), RT), :]
    w_hop(7)
    w_hop(8)
    for d in (1, 2, 3, 5, 6, 7, 4):
        j = lax.rem(g + 8 - d, 8)
        ref = att_recv.at[lax.div(j, 2), lax.rem(j, 2)]
        remote(ref, ref, a_ss.at[d - 1], a_rs.at[d - 1], grp(d)).wait_recv()
    for cc in range(2):
        for xx in range(4):
            att[cc, xx * RT : (xx + 1) * RT] = att_recv[lax.div(owner_s[2 * xx + cc, 0], 2), cc, xx]

    def core_copy(k):
        return remote(core_send.at[k], core_recv.at[k], c_ss.at[k], c_rs.at[k], sibling)

    def first(k, d):
        me, device = (x, along_x(d)) if k % 2 == 0 else (v, along_y(d))
        return remote(
            send1.at[k, lax.rem(me + d, 4)], recv1.at[k, d - 1], f_ss.at[k, d - 1], f_rs.at[k, d - 1], device
        )

    def second(k, d):
        me, device = (v, along_y(d)) if k % 2 == 0 else (x, along_x(d))
        return remote(
            send2.at[k, lax.rem(me + d, 4)], recv2.at[k, d - 1], g_ss.at[k, d - 1], g_rs.at[k, d - 1], device
        )

    def normed_copy(k, d, from_me=True):
        ref = hidden_c.at[k, v if from_me else lax.rem(v + 4 - d, 4)]
        return remote(ref, ref, n_ss.at[k, d - 1], n_rs.at[k, d - 1], along_y(d))

    def project(rows, k):
        columns = jnp.concatenate([w_slots[2 * k], w_slots[2 * k + 1]], axis=0)
        return lax.dot_general(rows, columns, (((1,), (1,)), ((), ())), preferred_element_type=F32)

    def to_sibling(k):
        core_send[k] = encode(project(att[1 - c], k))
        launch(core_copy(k))

    def step1(k):
        core_copy(k).wait_recv()
        total = project(att[c], k) + decode(core_recv[k])
        if k % 2 == 0:
            pieces = [total[i * 64 : (i + 1) * 64] for i in range(4)]
        else:
            pieces = [
                jnp.concatenate([total[j * 64 + i * 16 : j * 64 + i * 16 + 16] for j in range(4)], axis=0)
                for i in range(4)
            ]
        for i in range(4):
            tmp1[i] = pieces[i]
            send1[k, i] = encode(pieces[i])
        for d in (1, 3, 2):
            launch(first(k, d))
        own1[k] = tmp1[x if k % 2 == 0 else v]

    def step2(k):
        total = own1[k]
        for d in (1, 3, 2):
            first(k, d).wait_recv()
        for d in (1, 3, 2):
            total = total + decode(recv1[k, d - 1])
        coded = encode(total)
        for i in range(4):
            tmp2[i] = total[i * 16 : (i + 1) * 16]
            send2[k, i] = coded[i * 16 : (i + 1) * 16]
        for d in (1, 3, 2):
            launch(second(k, d))
        own2[k] = tmp2[v if k % 2 == 0 else x]

    def step3(k, square):
        cols = slice(k * CW, (k + 1) * CW)
        total = own2[k]
        for d in (1, 3, 2):
            second(k, d).wait_recv()
        for d in (1, 3, 2):
            total = total + decode(recv2[k, d - 1])
        hidden = resid_v[:, cols].astype(F32) + total
        for i in range(CW // 128):
            part = hidden[:, i * 128 : (i + 1) * 128]
            square = square + part * part
        hidden_c[k, v] = encode(hidden)
        for d in (1, 3, 2):
            launch(normed_copy(k, d))
        return square

    def step4(k, scale, logits):
        rows = decode(jnp.concatenate([hidden_c[k, i] for i in range(4)], axis=0))
        tiles = [
            (rows[:, i * 128 : (i + 1) * 128] * scale * gain_v[k * 5 + i : k * 5 + i + 1].astype(F32)).astype(BF)
            for i in range(CW // 128)
        ]
        return logits + lax.dot_general(
            head_v[:, k * CW : (k + 1) * CW], jnp.concatenate(tiles, axis=1), (((1,), (1,)), ((), ())),
            preferred_element_type=F32,
        )

    square = jnp.zeros((16, 128), F32)
    to_sibling(0)
    to_sibling(1)
    for k in range(4):
        to_sibling(k + 2)
        step1(k)
    for copy in late:
        copy.wait()
    for p in range(0, NCH, 2):
        if p + 4 < NCH:
            if p + 6 < NCH:
                to_sibling(p + 6)
                to_sibling(p + 7)
            step1(p + 4)
            step1(p + 5)
        step2(p)
        step2(p + 1)
        if p >= 2:
            square = step3(p - 2, square)
            square = step3(p - 1, square)
    square = step3(NCH - 2, square)
    square = step3(NCH - 1, square)
    squares[v] = square
    for d in (1, 3, 2):
        launch(remote(squares.at[v], squares.at[v], t_ss.at[d - 1], t_rs.at[d - 1], along_y(d)))
    for k in range(NCH):
        for d in (1, 3, 2):
            normed_copy(k, d, False).wait_recv()
    for d in (1, 3, 2):
        ref = squares.at[lax.rem(v + 4 - d, 4)]
        remote(ref, ref, t_ss.at[d - 1], t_rs.at[d - 1], along_y(d)).wait_recv()
    rows = jnp.concatenate([squares[i] for i in range(4)], axis=0)
    mean = jnp.broadcast_to(jnp.sum(rows, axis=1, keepdims=True) * (1.0 / D), (RT, 128))
    scale = lax.rsqrt(mean + 1e-06)
    logits = jnp.zeros((256, RT), F32)
    for k in range(NCH):
        logits = step4(k, scale, logits)

    high = jnp.max(logits, axis=0, keepdims=True)
    total = jnp.sum(jnp.exp(logits - high), axis=0, keepdims=True)
    entry = lax.broadcasted_iota(jnp.int32, (256, RT), 0) + v * 256
    picked = jnp.sum(jnp.where(entry == tok_v[0], logits, 0.0), axis=0, keepdims=True)
    stats[0, 0:1, 0:RT] = high
    stats[0, 1:2, 0:RT] = total
    stats[0, 2:3, 0:RT] = picked
    for d in (1, 3, 2):
        launch(remote(stats.at[0], stats.at[d], e_ss.at[d - 1], e_rs.at[d - 1], along_y(d)))
    for d in (1, 3, 2):
        remote(stats.at[0], stats.at[d], e_ss.at[d - 1], e_rs.at[d - 1], along_y(d)).wait_recv()
    highs = [high] + [stats[d, 0:1, 0:RT] for d in (1, 2, 3)]
    totals = [total] + [stats[d, 1:2, 0:RT] for d in (1, 2, 3)]
    target = picked + stats[1, 2:3, 0:RT] + stats[2, 2:3, 0:RT] + stats[3, 2:3, 0:RT]
    highest = functools.reduce(jnp.maximum, highs)
    exp_total = functools.reduce(jnp.add, [a * jnp.exp(b - highest) for a, b in zip(totals, highs)])
    logprob = target - (highest + jnp.log(exp_total))
    live = lax.broadcasted_iota(jnp.int32, (1, RT), 1) < len_s[0, 0]
    delta = jnp.clip(logprob - pol_v[0], -20.0, 20.0)
    divergence = jnp.clip(jnp.exp(delta) - delta - 1.0, -10.0, 10.0)
    ref_out[0] = jnp.where(live, logprob, 0.0)
    kl_out[0] = jnp.where(live, divergence, 0.0)
    for copy in sends:
        copy.wait_send()


def local(prompt_kv, owner, queries, resp_kv, lengths, out_proj, resid, gain, head_w, token_ids, pol_logprobs):
    vmem, hbm = pl.BlockSpec(memory_space=pltpu.VMEM), pl.BlockSpec(memory_space=pltpu.HBM)
    dma = pltpu.SemaphoreType.DMA
    wide = CW + 128
    scratch = [
        *[pltpu.VMEM((2, len(slots), 256, 128), BF) for slots in CHUNKS],
        pltpu.VMEM((4, 640, 128), BF),
        pltpu.VMEM((4, 256, 128), BF),
        pltpu.SMEM((1, 16), jnp.int32),
        pltpu.VMEM((8, 128), jnp.int32),
        pltpu.SMEM((8, 128), jnp.int32),
        pltpu.VMEM((4, 8, 512), F32),
        pltpu.VMEM((4, 8, 512), F32),
        pltpu.VMEM((4, STARTS[4], 512), F32),
        pltpu.VMEM((4, 512, 128), BF),
        pltpu.VMEM((4, 2, 4, RT, 128), BF),
        pltpu.VMEM((2, 256, 128), BF),
        pltpu.VMEM((128, 128), BF),
        pltpu.VMEM((16, 320, 128), BF),
        pltpu.VMEM((NCH, 256, wide), jnp.int16),
        pltpu.VMEM((NCH, 256, wide), jnp.int16),
        pltpu.VMEM((4, 64, CW), F32),
        pltpu.VMEM((NCH, 64, CW), F32),
        pltpu.VMEM((NCH, 4, 64, wide), jnp.int16),
        pltpu.VMEM((NCH, 3, 64, wide), jnp.int16),
        pltpu.VMEM((4, 16, CW), F32),
        pltpu.VMEM((NCH, 16, CW), F32),
        pltpu.VMEM((NCH, 4, 16, wide), jnp.int16),
        pltpu.VMEM((NCH, 3, 16, wide), jnp.int16),
        pltpu.VMEM((16, D), BF),
        pltpu.VMEM((256, D), BF),
        pltpu.VMEM((D // 128, 128), BF),
        pltpu.VMEM((1, 1, RT), jnp.int32),
        pltpu.VMEM((1, 1, RT), F32),
        pltpu.SMEM((1, 1), jnp.int32),
        pltpu.VMEM((NCH, 4, 16, wide), jnp.int16),
        pltpu.VMEM((4, 16, 128), F32),
        pltpu.VMEM((4, 8, 128), F32),
        dma((21,)),
    ]
    for shape in ((3,), (7,), (2, 8, 2), (16,), (2, 8), (7,), (NCH,), (NCH, 3), (NCH, 3), (NCH, 3), (3,), (3,)):
        scratch += [dma(shape), dma(shape)]
    out = jax.ShapeDtypeStruct((1, 1, RT), F32)
    return pl.pallas_call(
        kernel,
        out_shape=(out, out),
        in_specs=[hbm] * 11,
        out_specs=(vmem, vmem),
        scratch_shapes=scratch,
        compiler_params=pltpu.CompilerParams(
            collective_id=0, has_side_effects=True, vmem_limit_bytes=60 * 1024 * 1024
        ),
        name="score",
    )(
        prompt_kv, owner, queries, resp_kv, lengths, out_proj.T, resid, gain.reshape(D // 128, 128), head_w, token_ids,
        pol_logprobs,
    )


def solution(mesh):
    in_specs = (
        P("grp", "seq", "voc"),
        P("grp", None),
        P("grp", "seq", None, "voc"),
        P("grp", "seq", None, "voc"),
        P("grp", "seq"),
        P("voc", "seq"),
        P("grp", "seq", None, None),
        P(),
        P("voc", None),
        P("grp", "seq", None),
        P("grp", "seq", None),
    )
    out_specs = (P("grp", "seq", None), P("grp", "seq", None))
    return jax.shard_map(local, mesh=mesh, in_specs=in_specs, out_specs=out_specs, check_vma=False)
```

time: 278 us -> 107 us (0.38)
  waiting for transfers between devices: 199 us -> 0 us
  Pallas kernels: 0 us -> 103 us
  blocking collectives: 28.2 us -> 0 us
  between operations: 15.6 us -> 1.29 us
  matrix products: 11.5 us -> 0 us
  starting transfers between devices: 10 us -> 0 us
  other arithmetic: 6.29 us -> 0 us
  local copies, waits for them, and re-layouts: 5.5 us -> 2.25 us
    pallas_call x0 -> x1, Pallas kernels: none -> 103 us  [local(): pl.pallas_call(kernel, out_shape=(out, out), in_specs=[hbm] * 11, out_spe...]
    all_gather x1 -> x0, waiting for transfers between devices: 80.6 us -> none  [local(): lax.all_gather(out_proj, 'seq', axis=1, tiled=True)]
    all_to_all x1 -> x0, waiting for transfers between devices: 59.9 us -> none  [local(): lax.all_to_all(chosen, 'seq', split_axis=0, concat_axis=0, tiled=True)]
    psum x1 -> x0, waiting for transfers between devices: 57.4 us -> none  [local(): branch = lax.psum(partial_sum, 'voc')]
    all_gather x1 -> x0, blocking collectives: 20 us -> none  [local(): pieces = lax.all_gather(prompt_kv, 'grp', axis=0, tiled=True)]
    dot_general x4 -> x0, matrix products: 11.5 us -> none  [the longest x1 8.42 us: local(): jnp.dot(attention, lax.all_gather(out_proj, 'seq', axis=1, tiled=True), p...]
    all_to_all x1 -> x0, starting transfers between devices: 9.94 us -> none  [local(): lax.all_to_all(chosen, 'seq', split_axis=0, concat_axis=0, tiled=True)]
    unnamed x1 -> x0, blocking collectives: 8.22 us -> none
  transfers between devices with their start and end apart: 3 -> 0, of which waited for: 3 -> 0; matrix products, arithmetic and copies ran while one was open for 4% -> 0% of each run, Pallas kernels for 0% -> 0%
where the time goes in v1:
time: 107 us
  Pallas kernels  103 us (96%)
  local copies, waits for them, and re-layouts  2.25 us (2%)
  between operations  1.29 us (1%)
    pallas_call x1, Pallas kernels, local(): pl.pallas_call(kernel, out_shape=(out, out), in_specs=[hbm] * 11, out_spe...  103 us
    unnamed x2, local copies, waits for them, and re-layouts  2.25 us

profile of v1, /device:TPU:1, one launch (start us, length us, event | category | flops | bytes accessed | tf_op | source)
XLA Modules:
  0.0 106.7 jit_solution(9256316708119687495)
XLA Ops:
  1.3 103.2 %score.1 = (f32[1,1,64]{2,1,0:T(1,128)}, f32[1,1,64]{2,1,0:T(1,128)}) custom-call(bf16[1,128,256]{2,1,0:T(8,128)(2,1)} %kv_ref.1, s32[1,16]{1,0:T(1,128)} %owner_ref.1, bf16[1,1,64,1024]{3,2,1,0:T(8,128)(2,1)} %q_ref.1, bf16[1,1,64,256]{3,2,1,0:T(8,128)(2,1)} %own_ref.1, s32[1,1]{1,0:T(1,128)S(6)} %copy.15.len_ref, bf16[320,1024]{1,0:T(8,128)(2,1)} %bitcast.2, ...), custom_call_target="tpu_custom_call" | custom-call | tf_op jit(solution)/shard_map/score/pallas_call | solution.py:478
  104.4 1.1 %copy.16 = f32[1,1,64]{2,1,0:T(1,128)} copy(f32[1,1,64]{2,1,0:T(1,128)} %get-tuple-element.4) | data formatting | bytes 512
  105.5 1.1 %copy.17 = f32[1,1,64]{2,1,0:T(1,128)} copy(f32[1,1,64]{2,1,0:T(1,128)} %get-tuple-element.5) | data formatting | bytes 512

commit v2 on v1

--- a/solution.py
+++ b/solution.py
@@ -17,8 +17,10 @@
 BF = jnp.bfloat16
 F32 = jnp.float32
 LOG2E_SCALE = math.log2(math.e) / math.sqrt(HD)
-CHUNKS = ((0, 1, 2), (3, 4, 5, 6), (7, 8, 9, 10), (11, 12, 13, 14, 15))
-STARTS = (0, 512, 1024, 1536, 2176)
+CHUNKS = ((0, 1, 2, 3, 4), (5, 6, 7, 8), (9, 10, 11, 12), (13, 14, 15))
+STARTS = (0, 768, 1280, 1792, 2176)
+X_FIRST = (False, True, False, True, True, True, True, True)
+ORDER = (0, 1, 7, 2, 6, 3, 5, 4)
 PLACE = {slot: (t, i) for t, slots in enumerate(CHUNKS) for i, slot in enumerate(slots)}
 
 
@@ -46,12 +48,12 @@
 
 
 def kernel(
-    kv_ref, owner_ref, q_ref, own_ref, len_ref, proj_ref, resid_ref, gain_ref, head_ref, tok_ref, pol_ref,
-    ref_out, kl_out,
+    kv_ref, owner_ref, q_ref, own_ref, proj_ref, resid_ref, gain_ref, head_ref, tok_ref, pol_ref,
+    out_ref,
     kv0, kv1, kv2, kv3, packs, own_blocks, owner_in, owner_v, owner_s, m_s, l_s, probs, att_send, att_recv, att,
-    v_in, w_slots, core_send, core_recv, tmp1, own1, send1, recv1, tmp2, own2, send2, recv2,
-    resid_v, head_v, gain_v, tok_v, pol_v, len_s, hidden_c, squares, stats, load_sem,
-    q_ss, q_rs, o_ss, o_rs, kv_ss, kv_rs, sib_ss, sib_rs, w_ss, w_rs, a_ss, a_rs, c_ss, c_rs,
+    v_in, w_slots, tmp1, own1, kept, send1, recv1, tmp2, own2, send2, recv2,
+    resid_v, head_v, gain_in, gain_v, tok_v, pol_v, hidden_c, hidden_v, squares, stats, load_sem,
+    q_ss, q_rs, o_ss, o_rs, kv_ss, kv_rs, sib_ss, sib_rs, w_ss, w_rs, wb_ss, wb_rs, a_ss, a_rs,
     f_ss, f_rs, g_ss, g_rs, n_ss, n_rs, t_ss, t_rs, e_ss, e_rs,
 ):
     g, s, v = lax.axis_index("grp"), lax.axis_index("seq"), lax.axis_index("voc")
@@ -68,9 +70,6 @@
         copy.start()
         sends.append(copy)
 
-    def grp(d):
-        return {"grp": lax.rem(g + d, 8)}
-
     def along_x(d):
         return {"grp": lax.rem(g + 2 * d, 8)}
 
@@ -83,7 +82,7 @@
     sibling = {"grp": 2 * x + 1 - c}
 
     barrier = pltpu.get_barrier_semaphore()
-    for device in [grp(d) for d in range(1, 8)] + [along_y(d) for d in range(1, 4)] + [along_z(0), along_z(1)]:
+    for device in [along_x(d) for d in range(1, 4)] + [along_y(d) for d in range(1, 4)] + [along_z(0), along_z(1), sibling]:
         pl.semaphore_signal(barrier, inc=1, device_id=device, device_id_type=MESH)
 
     def load(index, src, dst):
@@ -92,27 +91,25 @@
         return copy
 
     early = [
-        load(0, owner_ref, owner_in),
         load(1, kv_ref.at[0, :, pl.ds(HD, HD)], v_in),
         load(2, kv_ref.at[0, :, pl.ds(0, HD)], kv0.at[c, 0, pl.ds(0, HD)]),
     ]
-    early += [load(3 + j, q_ref.at[0, 0, :, pl.ds(j * HD, HD)], packs.at[x, pl.ds(j * RT, RT)]) for j in range(8)]
-    early += [load(11 + j, own_ref.at[0, 0, :, pl.ds(j * HD, HD)], packs.at[x, pl.ds(512 + j * RT, RT)]) for j in range(2)]
-    early.append(load(13, proj_ref.at[:, pl.ds(pl.multiple_of(g * HD, HD), HD)], w_slots.at[s]))
+    early_owner = load(0, owner_ref, owner_in)
+    early_q = [load(3 + j, q_ref.at[0, 0, :, pl.ds(j * HD, HD)], packs.at[x, pl.ds(j * RT, RT)]) for j in range(8)]
+    early_q += [load(11 + j, own_ref.at[0, 0, :, pl.ds(j * HD, HD)], packs.at[x, pl.ds(512 + j * RT, RT)]) for j in range(2)]
+    early_w = load(13, proj_ref.at[:, pl.ds(pl.multiple_of(g * HD, HD), HD)], w_slots.at[c, s])
     late = [
         load(14, resid_ref.at[0, 0, pl.ds(pl.multiple_of(v * 16, 16), 16), :], resid_v),
         load(15, head_ref, head_v),
-        load(16, gain_ref, gain_v),
+        load(16, gain_ref, gain_in),
         load(17, tok_ref, tok_v),
         load(18, pol_ref, pol_v),
-        load(19, len_ref, len_s),
     ]
     for copy in early:
         copy.wait()
     kv0[c, 0, 128:256] = v_in[...].T
-    owner_v[pl.ds(g, 1), :] = jnp.full((1, 128), owner_in[0, s], jnp.int32)
-
-    pl.semaphore_wait(barrier, 12)
+
+    pl.semaphore_wait(barrier, 9)
 
     def kv_piece(slot, sub):
         t, i = PLACE[slot]
@@ -144,8 +141,8 @@
     def w_piece(way, hop, which):
         index = lax.rem(s + (16 - hop if way == 0 else hop), 16)
         if which == 8:
-            return w_slots.at[index, pl.ds(way * 160, 160)]
-        return w_slots.at[index]
+            return w_slots.at[c, index, pl.ds(way * 160, 160)]
+        return w_slots.at[c, index]
 
     def w_copy(way, hop):
         return remote(
@@ -162,23 +159,39 @@
             w_arrived(way, hop).wait_recv()
             if hop < 8:
                 launch(w_copy(way, hop + 1))
+        for way in (0, 1) if hop < 8 else (0,):
+            launch(w_sib(way, hop, c))
+
+    def w_sib(way, hop, head):
+        ref = w_slots.at[head, lax.rem(s + (16 - hop if way == 0 else hop), 16)]
+        slot = slot_of(way, hop)
+        return remote(ref, ref, wb_ss.at[slot], wb_rs.at[slot], sibling)
+
+    def w_ready(hop):
+        for way in (0, 1) if 0 < hop < 8 else (0,):
+            w_sib(way, hop, 1 - c).wait_recv()
 
     for sub in (0, 1):
         for way in (0, 1):
             launch(kv_copy(way, 1, sub))
     launch(sib_copy(0))
-    for d in range(1, 8):
+    for copy in early_q:
+        copy.wait()
+    for d in (1, 3, 2):
+        launch(remote(packs.at[x], packs.at[x], q_ss.at[d - 1], q_rs.at[d - 1], along_x(d)))
+    early_owner.wait()
+    owner_v[pl.ds(g, 1), :] = jnp.full((1, 128), owner_in[0, s], jnp.int32)
+    for d in (1, 3, 2):
         row = owner_v.at[pl.ds(g, 1)]
-        launch(remote(row, row, o_ss.at[d - 1], o_rs.at[d - 1], grp(d)))
-    for d in (1, 3, 2):
-        launch(remote(packs.at[x], packs.at[x], q_ss.at[d - 1], q_rs.at[d - 1], along_x(d)))
+        launch(remote(row, row, o_ss.at[d - 1], o_rs.at[d - 1], along_x(d)))
 
     kv_hop(1)
     kv_hop(2)
-
-    for d in range(1, 8):
-        row = owner_v.at[pl.ds(lax.rem(g + 8 - d, 8), 1)]
-        remote(row, row, o_ss.at[d - 1], o_rs.at[d - 1], grp(d)).wait_recv()
+    kv_hop(3)
+
+    for d in (1, 3, 2):
+        row = owner_v.at[pl.ds(lax.rem(g + 8 - 2 * d, 8), 1)]
+        remote(row, row, o_ss.at[d - 1], o_rs.at[d - 1], along_x(d)).wait_recv()
     to_scalar = pltpu.make_async_copy(owner_v, owner_s, load_sem.at[20])
     to_scalar.start()
     for d in (1, 3, 2):
@@ -237,63 +250,60 @@
             sib_ref = kvs[t].at[1 - c, PLACE[slot][1]]
             remote(sib_ref, sib_ref, sib_ss.at[slot], sib_rs.at[slot], sibling).wait_recv()
 
+    kv_hop(4)
+    chunk_ready(0)
+    attend(0, (0, 1))
+    kv_hop(5)
+    attend(0, (2, 3))
+    early_w.wait()
     for way in (0, 1):
         launch(w_copy(way, 1))
-    kv_hop(3)
-    chunk_ready(0)
-    attend(0, (0, 1))
-    kv_hop(4)
-    attend(0, (2, 3))
-    w_hop(1)
-    kv_hop(5)
+    launch(w_sib(0, 0, c))
+    kv_hop(6)
     chunk_ready(1)
     attend(1, (0, 1))
+    kv_hop(7)
+    attend(1, (2, 3))
+    w_hop(1)
+    kv_hop(8)
+    chunk_ready(2)
+    attend(2, (0, 1, 2, 3))
     w_hop(2)
-    kv_hop(6)
-    attend(1, (2, 3))
-    w_hop(3)
-    kv_hop(7)
-    chunk_ready(2)
-    attend(2, (0, 1))
-    w_hop(4)
-    kv_hop(8)
-    attend(2, (2, 3))
-    w_hop(5)
     chunk_ready(3)
-    attend(3, (0, 1))
-    w_hop(6)
-    attend(3, (2, 3))
-
+    attend(3, (0, 1, 2, 3))
+
+    def att_copy(d, half):
+        heads = pl.ds(pl.multiple_of(lax.rem(x + d, 4) * 2 * RT, 2 * RT), 2 * RT)
+        return remote(
+            att_send.at[pl.ds(2 * half, 2), heads, :], att_recv.at[x, pl.ds(2 * half, 2)],
+            a_ss.at[d - 1, half], a_rs.at[d - 1, half], along_x(d),
+        )
+
+    for half in (0, 1):
+        weigh(2 * half)
+        weigh(2 * half + 1)
+        for d in (2, 1, 3):
+            launch(att_copy(d, half))
+        w_hop(3 + half)
+    att_recv[x] = att_send[:, pl.ds(pl.multiple_of(x * 2 * RT, 2 * RT), 2 * RT), :]
+    for half in (0, 1):
+        for d in (1, 3, 2):
+            ref = att_recv.at[lax.rem(x + 4 - d, 4), pl.ds(2 * half, 2)]
+            remote(ref, ref, a_ss.at[d - 1, half], a_rs.at[d - 1, half], along_x(d)).wait_recv()
     for u in range(4):
-        weigh(u)
-    for d in (1, 2, 3, 5, 6, 7, 4):
-        j = lax.rem(g + d, 8)
-        launch(remote(
-            att_send.at[:, pl.ds(pl.multiple_of(j * RT, RT), RT), :], att_recv.at[x, c],
-            a_ss.at[d - 1], a_rs.at[d - 1], grp(d),
-        ))
-    att_recv[x, c] = att_send[:, pl.ds(pl.multiple_of(g * RT, RT), RT), :]
-    w_hop(7)
-    w_hop(8)
-    for d in (1, 2, 3, 5, 6, 7, 4):
-        j = lax.rem(g + 8 - d, 8)
-        ref = att_recv.at[lax.div(j, 2), lax.rem(j, 2)]
-        remote(ref, ref, a_ss.at[d - 1], a_rs.at[d - 1], grp(d)).wait_recv()
-    for cc in range(2):
-        for xx in range(4):
-            att[cc, xx * RT : (xx + 1) * RT] = att_recv[lax.div(owner_s[2 * xx + cc, 0], 2), cc, xx]
-
-    def core_copy(k):
-        return remote(core_send.at[k], core_recv.at[k], c_ss.at[k], c_rs.at[k], sibling)
-
-    def first(k, d):
-        me, device = (x, along_x(d)) if k % 2 == 0 else (v, along_y(d))
+        heads = att_recv[lax.div(owner_s[2 * u + c, 0], 2), u]
+        for h in (0, 1):
+            att[h, u * RT : (u + 1) * RT] = heads[h * RT : (h + 1) * RT]
+
+    def first(k, kind):
+        step = 1 if kind < 3 else 3
         return remote(
-            send1.at[k, lax.rem(me + d, 4)], recv1.at[k, d - 1], f_ss.at[k, d - 1], f_rs.at[k, d - 1], device
+            send1.at[k, kind], recv1.at[k, kind], f_ss.at[k, kind], f_rs.at[k, kind],
+            along_x(step) if X_FIRST[k] else along_y(step),
         )
 
     def second(k, d):
-        me, device = (v, along_y(d)) if k % 2 == 0 else (x, along_x(d))
+        me, device = (v, along_y(d)) if X_FIRST[k] else (x, along_x(d))
         return remote(
             send2.at[k, lax.rem(me + d, 4)], recv2.at[k, d - 1], g_ss.at[k, d - 1], g_rs.at[k, d - 1], device
         )
@@ -302,18 +312,19 @@
         ref = hidden_c.at[k, v if from_me else lax.rem(v + 4 - d, 4)]
         return remote(ref, ref, n_ss.at[k, d - 1], n_rs.at[k, d - 1], along_y(d))
 
-    def project(rows, k):
-        columns = jnp.concatenate([w_slots[2 * k], w_slots[2 * k + 1]], axis=0)
-        return lax.dot_general(rows, columns, (((1,), (1,)), ((), ())), preferred_element_type=F32)
-
-    def to_sibling(k):
-        core_send[k] = encode(project(att[1 - c], k))
-        launch(core_copy(k))
+    def chunk(k):
+        return lax.rem(lax.div(s, 2) + ORDER[k], 8)
+
+    def columns_of(k):
+        return pl.ds(pl.multiple_of(chunk(k) * CW, CW), CW)
+
+    def project(h, k):
+        columns = jnp.concatenate([w_slots[h, 2 * chunk(k)], w_slots[h, 2 * chunk(k) + 1]], axis=0)
+        return lax.dot_general(att[h], columns, (((1,), (1,)), ((), ())), preferred_element_type=F32)
 
     def step1(k):
-        core_copy(k).wait_recv()
-        total = project(att[c], k) + decode(core_recv[k])
-        if k % 2 == 0:
+        total = project(0, k) + project(1, k)
+        if X_FIRST[k]:
             pieces = [total[i * 64 : (i + 1) * 64] for i in range(4)]
         else:
             pieces = [
@@ -322,33 +333,44 @@
             ]
         for i in range(4):
             tmp1[i] = pieces[i]
-            send1[k, i] = encode(pieces[i])
-        for d in (1, 3, 2):
-            launch(first(k, d))
-        own1[k] = tmp1[x if k % 2 == 0 else v]
+        me = x if X_FIRST[k] else v
+        after, opposite, before = lax.rem(me + 1, 4), lax.rem(me + 2, 4), lax.rem(me + 3, 4)
+        for kind, piece, rows in (
+            (0, opposite, slice(0, 32)), (3, opposite, slice(32, 64)), (1, after, slice(32, 64)), (4, before, slice(0, 32))
+        ):
+            send1[k, kind] = encode(tmp1[piece, rows])
+            launch(first(k, kind))
+        kept[k, 0:32] = tmp1[after, 0:32]
+        kept[k, 32:64] = tmp1[before, 32:64]
+        own1[k] = tmp1[me]
+
+    def relay(k):
+        for kind, rows in ((0, slice(0, 32)), (3, slice(32, 64))):
+            first(k, kind).wait_recv()
+            send1[k, kind + 2] = encode(kept[k, rows] + decode(recv1[k, kind]))
+            launch(first(k, kind + 2))
 
     def step2(k):
-        total = own1[k]
-        for d in (1, 3, 2):
-            first(k, d).wait_recv()
-        for d in (1, 3, 2):
-            total = total + decode(recv1[k, d - 1])
+        for kind in (1, 4, 2, 5):
+            first(k, kind).wait_recv()
+        total = own1[k] + jnp.concatenate(
+            [decode(recv1[k, 4]) + decode(recv1[k, 2]), decode(recv1[k, 1]) + decode(recv1[k, 5])], axis=0
+        )
         coded = encode(total)
         for i in range(4):
             tmp2[i] = total[i * 16 : (i + 1) * 16]
             send2[k, i] = coded[i * 16 : (i + 1) * 16]
         for d in (1, 3, 2):
             launch(second(k, d))
-        own2[k] = tmp2[v if k % 2 == 0 else x]
+        own2[k] = tmp2[v if X_FIRST[k] else x]
 
     def step3(k, square):
-        cols = slice(k * CW, (k + 1) * CW)
         total = own2[k]
         for d in (1, 3, 2):
             second(k, d).wait_recv()
         for d in (1, 3, 2):
             total = total + decode(recv2[k, d - 1])
-        hidden = resid_v[:, cols].astype(F32) + total
+        hidden = resid_v[:, columns_of(k)].astype(F32) + total
         for i in range(CW // 128):
             part = hidden[:, i * 128 : (i + 1) * 128]
             square = square + part * part
@@ -357,45 +379,77 @@
             launch(normed_copy(k, d))
         return square
 
-    def step4(k, scale, logits):
-        rows = decode(jnp.concatenate([hidden_c[k, i] for i in range(4)], axis=0))
+    def step4(k):
+        for d in (1, 3, 2):
+            normed_copy(k, d, False).wait_recv()
+        hidden_v[k] = decode(jnp.concatenate([hidden_c[k, i] for i in range(4)], axis=0))
+
+    def step5(k, scale, logits):
         tiles = [
-            (rows[:, i * 128 : (i + 1) * 128] * scale * gain_v[k * 5 + i : k * 5 + i + 1].astype(F32)).astype(BF)
+            (hidden_v[k, :, i * 128 : (i + 1) * 128] * scale * gain_v[chunk(k), i : i + 1]).astype(BF)
             for i in range(CW // 128)
         ]
         return logits + lax.dot_general(
-            head_v[:, k * CW : (k + 1) * CW], jnp.concatenate(tiles, axis=1), (((1,), (1,)), ((), ())),
+            head_v[:, columns_of(k)], jnp.concatenate(tiles, axis=1), (((1,), (1,)), ((), ())),
             preferred_element_type=F32,
         )
 
     square = jnp.zeros((16, 128), F32)
-    to_sibling(0)
-    to_sibling(1)
-    for k in range(4):
-        to_sibling(k + 2)
-        step1(k)
+    for hop in (0, 1):
+        w_ready(hop)
+    step1(0)
+    for hop in (2, 3):
+        w_ready(hop)
+    step1(1)
+    w_hop(5)
+    step1(2)
+    relay(0)
+    for hop in (4, 5):
+        w_ready(hop)
+    step1(3)
+    w_hop(6)
+    relay(1)
+    step1(4)
+    relay(2)
+    w_hop(7)
     for copy in late:
         copy.wait()
-    for p in range(0, NCH, 2):
-        if p + 4 < NCH:
-            if p + 6 < NCH:
-                to_sibling(p + 6)
-                to_sibling(p + 7)
-            step1(p + 4)
-            step1(p + 5)
-        step2(p)
-        step2(p + 1)
-        if p >= 2:
-            square = step3(p - 2, square)
-            square = step3(p - 1, square)
-    square = step3(NCH - 2, square)
+    for i in range(NCH):
+        gain_v[i, 0:5] = gain_in[i * 5 : i * 5 + 5].astype(F32)
+    step2(0)
+    relay(3)
+    step2(1)
+    for hop in (6, 7):
+        w_ready(hop)
+    step1(5)
+    step2(2)
+    w_hop(8)
+    square = step3(0, square)
+    relay(4)
+    step2(3)
+    step1(6)
+    square = step3(1, square)
+    square = step3(2, square)
+    relay(5)
+    step2(4)
+    w_ready(8)
+    step1(7)
+    square = step3(3, square)
+    step4(0)
+    step4(1)
+    step4(2)
+    for k in range(5, NCH):
+        if k + 1 < NCH:
+            relay(k + 1)
+        step2(k)
+        square = step3(k - 1, square)
+        step4(k - 2)
     square = step3(NCH - 1, square)
     squares[v] = square
     for d in (1, 3, 2):
         launch(remote(squares.at[v], squares.at[v], t_ss.at[d - 1], t_rs.at[d - 1], along_y(d)))
-    for k in range(NCH):
-        for d in (1, 3, 2):
-            normed_copy(k, d, False).wait_recv()
+    step4(6)
+    step4(7)
     for d in (1, 3, 2):
         ref = squares.at[lax.rem(v + 4 - d, 4)]
         remote(ref, ref, t_ss.at[d - 1], t_rs.at[d - 1], along_y(d)).wait_recv()
@@ -404,7 +458,7 @@
     scale = lax.rsqrt(mean + 1e-06)
     logits = jnp.zeros((256, RT), F32)
     for k in range(NCH):
-        logits = step4(k, scale, logits)
+        logits = step5(k, scale, logits)
 
     high = jnp.max(logits, axis=0, keepdims=True)
     total = jnp.sum(jnp.exp(logits - high), axis=0, keepdims=True)
@@ -423,11 +477,10 @@
     highest = functools.reduce(jnp.maximum, highs)
     exp_total = functools.reduce(jnp.add, [a * jnp.exp(b - highest) for a, b in zip(totals, highs)])
     logprob = target - (highest + jnp.log(exp_total))
-    live = lax.broadcasted_iota(jnp.int32, (1, RT), 1) < len_s[0, 0]
     delta = jnp.clip(logprob - pol_v[0], -20.0, 20.0)
     divergence = jnp.clip(jnp.exp(delta) - delta - 1.0, -10.0, 10.0)
-    ref_out[0] = jnp.where(live, logprob, 0.0)
-    kl_out[0] = jnp.where(live, divergence, 0.0)
+    out_ref[0, 0:1] = logprob
+    out_ref[0, 1:2] = divergence
     for copy in sends:
         copy.wait_send()
 
@@ -447,16 +500,15 @@
         pltpu.VMEM((4, 8, 512), F32),
         pltpu.VMEM((4, STARTS[4], 512), F32),
         pltpu.VMEM((4, 512, 128), BF),
-        pltpu.VMEM((4, 2, 4, RT, 128), BF),
+        pltpu.VMEM((4, 4, 2 * RT, 128), BF),
         pltpu.VMEM((2, 256, 128), BF),
         pltpu.VMEM((128, 128), BF),
-        pltpu.VMEM((16, 320, 128), BF),
-        pltpu.VMEM((NCH, 256, wide), jnp.int16),
-        pltpu.VMEM((NCH, 256, wide), jnp.int16),
+        pltpu.VMEM((2, 16, 320, 128), BF),
         pltpu.VMEM((4, 64, CW), F32),
         pltpu.VMEM((NCH, 64, CW), F32),
-        pltpu.VMEM((NCH, 4, 64, wide), jnp.int16),
-        pltpu.VMEM((NCH, 3, 64, wide), jnp.int16),
+        pltpu.VMEM((NCH, 64, CW), F32),
+        pltpu.VMEM((NCH, 6, 32, wide), jnp.int16),
+        pltpu.VMEM((NCH, 6, 32, wide), jnp.int16),
         pltpu.VMEM((4, 16, CW), F32),
         pltpu.VMEM((NCH, 16, CW), F32),
         pltpu.VMEM((NCH, 4, 16, wide), jnp.int16),
@@ -464,31 +516,33 @@
         pltpu.VMEM((16, D), BF),
         pltpu.VMEM((256, D), BF),
         pltpu.VMEM((D // 128, 128), BF),
+        pltpu.VMEM((NCH, 8, 128), F32),
         pltpu.VMEM((1, 1, RT), jnp.int32),
         pltpu.VMEM((1, 1, RT), F32),
-        pltpu.SMEM((1, 1), jnp.int32),
         pltpu.VMEM((NCH, 4, 16, wide), jnp.int16),
+        pltpu.VMEM((NCH, RT, CW), F32),
         pltpu.VMEM((4, 16, 128), F32),
         pltpu.VMEM((4, 8, 128), F32),
         dma((21,)),
     ]
-    for shape in ((3,), (7,), (2, 8, 2), (16,), (2, 8), (7,), (NCH,), (NCH, 3), (NCH, 3), (NCH, 3), (3,), (3,)):
+    for shape in ((3,), (3,), (2, 8, 2), (16,), (2, 8), (16,), (3, 2), (NCH, 6), (NCH, 3), (NCH, 3), (3,), (3,)):
         scratch += [dma(shape), dma(shape)]
-    out = jax.ShapeDtypeStruct((1, 1, RT), F32)
-    return pl.pallas_call(
+    scored = pl.pallas_call(
         kernel,
-        out_shape=(out, out),
-        in_specs=[hbm] * 11,
-        out_specs=(vmem, vmem),
+        out_shape=jax.ShapeDtypeStruct((1, 2, RT), F32),
+        in_specs=[hbm] * 10,
+        out_specs=vmem,
         scratch_shapes=scratch,
         compiler_params=pltpu.CompilerParams(
             collective_id=0, has_side_effects=True, vmem_limit_bytes=60 * 1024 * 1024
         ),
         name="score",
     )(
-        prompt_kv, owner, queries, resp_kv, lengths, out_proj.T, resid, gain.reshape(D // 128, 128), head_w, token_ids,
+        prompt_kv, owner, queries, resp_kv, out_proj.T, resid, gain.reshape(D // 128, 128), head_w, token_ids,
         pol_logprobs,
     )
+    live = lax.broadcasted_iota(jnp.int32, (1, 1, RT), 2) < lengths[0, 0]
+    return jnp.where(live, scored[:, 0:1], 0.0), jnp.where(live, scored[:, 1:2], 0.0)
 
 
 def solution(mesh):

time: 107 us -> 99.9 us (0.934)
  the two profiles are of different devices: /device:TPU:1 before, /device:TPU:32 now
where the time goes in v2:
time: 99.9 us; the launch traced here: 99.8 us
  Pallas kernels  97.2 us (97%)
  between operations  1.29 us (1%)
  other arithmetic  1.26 us (1%)
    pallas_call x1, Pallas kernels, local(): pl.pallas_call(kernel, out_shape=jax.ShapeDtypeStruct((1, 2, RT), F32), i...  97.2 us

profile of v2, /device:TPU:32, one launch (start us, length us, event | category | flops | bytes accessed | tf_op | source)
XLA Modules:
  0.0 99.8 jit_solution(13338296643417601466)
XLA Ops:
  1.3 97.2 %score.1 = f32[1,2,64]{2,1,0:T(2,128)} custom-call(bf16[1,128,256]{2,1,0:T(8,128)(2,1)} %kv_ref.1, s32[1,16]{1,0:T(1,128)} %owner_ref.1, bf16[1,1,64,1024]{3,2,1,0:T(8,128)(2,1)} %q_ref.1, bf16[1,1,64,256]{3,2,1,0:T(8,128)(2,1)} %own_ref.1, bf16[320,1024]{1,0:T(8,128)(2,1)} %bitcast.4, bf16[1,1,64,5120]{3,2,1,0:T(8,128)(2,1)} %resid_ref.1, ...), custom_call_target="tpu_custom_call" | custom-call | tf_op jit(solution)/shard_map/score/pallas_call | solution.py:530
  98.5 1.3 %compare_select_fusion = (f32[1,1,64]{2,1,0:T(1,128)}, f32[1,1,64]{2,1,0:T(1,128)}) fusion(f32[1,2,64]{2,1,0:T(2,128)} %score.1, s32[]{:T(128)} %bitcast.3), kind=kLoop, calls=%fused_computation | loop fusion | flops 192 | bytes 1028 | tf_op jit(solution)/shard_map/jit(_where)/select_n | solution.py:545

commit v3 on v2

--- a/solution.py
+++ b/solution.py
@@ -19,7 +19,7 @@
 LOG2E_SCALE = math.log2(math.e) / math.sqrt(HD)
 CHUNKS = ((0, 1, 2, 3, 4), (5, 6, 7, 8), (9, 10, 11, 12), (13, 14, 15))
 STARTS = (0, 768, 1280, 1792, 2176)
-X_FIRST = (False, True, False, True, True, True, True, True)
+X_FIRST = (False, True, False, True, True, False, True, True)
 ORDER = (0, 1, 7, 2, 6, 3, 5, 4)
 PLACE = {slot: (t, i) for t, slots in enumerate(CHUNKS) for i, slot in enumerate(slots)}
 
@@ -35,16 +35,43 @@
     return jnp.broadcast_to(jnp.max(high, axis=1, keepdims=True), high.shape)
 
 
-def encode(rows):
+def scaled_rows(rows):
     exponent = jnp.ceil(jnp.log2(jnp.maximum(lanes_max(rows), 1e-30)) + 0.01)
     scale = jnp.exp2(-exponent) * 32000.0
-    scaled = rows * jnp.concatenate([scale] * (CW // 128), axis=1)
-    return jnp.concatenate([jnp.round(scaled), exponent], axis=1).astype(jnp.int16)
+    return jnp.round(rows * jnp.concatenate([scale] * (CW // 128), axis=1)), exponent
+
+
+def restored(values, exponent):
+    scale = jnp.exp2(exponent) * (1.0 / 32000.0)
+    return values.astype(F32) * jnp.concatenate([scale] * (CW // 128), axis=1)
+
+
+def encode(rows):
+    return jnp.concatenate(scaled_rows(rows), axis=1).astype(jnp.int16)
 
 
 def decode(coded):
-    scale = jnp.exp2(coded[:, CW:].astype(F32)) * (1.0 / 32000.0)
-    return coded[:, :CW].astype(F32) * jnp.concatenate([scale] * (CW // 128), axis=1)
+    return restored(coded[:, :CW], coded[:, CW:].astype(F32))
+
+
+def encode_pair(rows):
+    values, exponent = scaled_rows(rows)
+    left = lax.broadcasted_iota(jnp.int32, (16, 128), 1) < 64
+    both = jnp.where(left, exponent[0:16], exponent[16:32])
+    return jnp.concatenate([values[0:16], values[16:32], both], axis=1).astype(jnp.int16)
+
+
+def decode_pair(coded):
+    both = coded[:, 2 * CW :].astype(F32)
+    turned = jnp.concatenate([both[:, 64:], both[:, :64]], axis=1)
+    left = lax.broadcasted_iota(jnp.int32, (16, 128), 1) < 64
+    return jnp.concatenate(
+        [
+            restored(coded[:, :CW], jnp.where(left, both, turned)),
+            restored(coded[:, CW : 2 * CW], jnp.where(left, turned, both)),
+        ],
+        axis=0,
+    )
 
 
 def kernel(
@@ -338,7 +365,7 @@
         for kind, piece, rows in (
             (0, opposite, slice(0, 32)), (3, opposite, slice(32, 64)), (1, after, slice(32, 64)), (4, before, slice(0, 32))
         ):
-            send1[k, kind] = encode(tmp1[piece, rows])
+            send1[k, kind] = encode_pair(tmp1[piece, rows])
             launch(first(k, kind))
         kept[k, 0:32] = tmp1[after, 0:32]
         kept[k, 32:64] = tmp1[before, 32:64]
@@ -347,14 +374,14 @@
     def relay(k):
         for kind, rows in ((0, slice(0, 32)), (3, slice(32, 64))):
             first(k, kind).wait_recv()
-            send1[k, kind + 2] = encode(kept[k, rows] + decode(recv1[k, kind]))
+            send1[k, kind + 2] = encode_pair(kept[k, rows] + decode_pair(recv1[k, kind]))
             launch(first(k, kind + 2))
 
     def step2(k):
         for kind in (1, 4, 2, 5):
             first(k, kind).wait_recv()
         total = own1[k] + jnp.concatenate(
-            [decode(recv1[k, 4]) + decode(recv1[k, 2]), decode(recv1[k, 1]) + decode(recv1[k, 5])], axis=0
+            [decode_pair(recv1[k, 4]) + decode_pair(recv1[k, 2]), decode_pair(recv1[k, 1]) + decode_pair(recv1[k, 5])], axis=0
         )
         coded = encode(total)
         for i in range(4):
@@ -507,8 +534,8 @@
         pltpu.VMEM((4, 64, CW), F32),
         pltpu.VMEM((NCH, 64, CW), F32),
         pltpu.VMEM((NCH, 64, CW), F32),
-        pltpu.VMEM((NCH, 6, 32, wide), jnp.int16),
-        pltpu.VMEM((NCH, 6, 32, wide), jnp.int16),
+        pltpu.VMEM((NCH, 6, 16, 2 * CW + 128), jnp.int16),
+        pltpu.VMEM((NCH, 6, 16, 2 * CW + 128), jnp.int16),
         pltpu.VMEM((4, 16, CW), F32),
         pltpu.VMEM((NCH, 16, CW), F32),
         pltpu.VMEM((NCH, 4, 16, wide), jnp.int16),

time: 99.9 us -> 99 us (level)
  the two profiles are of different devices: /device:TPU:32 before, /device:TPU:1 now
where the time goes in v3:
time: 99 us; the launch traced here: 98 us
  Pallas kernels  95.4 us (96%)
  between operations  1.29 us (1%)
  other arithmetic  1.26 us (1%)
    pallas_call x1, Pallas kernels, local(): pl.pallas_call(kernel, out_shape=jax.ShapeDtypeStruct((1, 2, RT), F32), i...  95.4 us

profile of v3, /device:TPU:1, one launch (start us, length us, event | category | flops | bytes accessed | tf_op | source)
XLA Modules:
  0.0 98.0 jit_solution(5090110773920601892)
XLA Ops:
  1.3 95.4 %score.1 = f32[1,2,64]{2,1,0:T(2,128)} custom-call(bf16[1,128,256]{2,1,0:T(8,128)(2,1)} %kv_ref.1, s32[1,16]{1,0:T(1,128)} %owner_ref.1, bf16[1,1,64,1024]{3,2,1,0:T(8,128)(2,1)} %q_ref.1, bf16[1,1,64,256]{3,2,1,0:T(8,128)(2,1)} %own_ref.1, bf16[320,1024]{1,0:T(8,128)(2,1)} %bitcast.4, bf16[1,1,64,5120]{3,2,1,0:T(8,128)(2,1)} %resid_ref.1, ...), custom_call_target="tpu_custom_call" | custom-call | tf_op jit(solution)/shard_map/score/pallas_call | solution.py:557
  96.7 1.3 %compare_select_fusion = (f32[1,1,64]{2,1,0:T(1,128)}, f32[1,1,64]{2,1,0:T(1,128)}) fusion(f32[1,2,64]{2,1,0:T(2,128)} %score.1, s32[]{:T(128)} %bitcast.3), kind=kLoop, calls=%fused_computation | loop fusion | flops 192 | bytes 1028 | tf_op jit(solution)/shard_map/jit(_where)/select_n | solution.py:572
